TPU v7x, 256 devices: a whole 4x4x8 slice. The times are simulated.
256 devices in a mesh: row: 16 (over y, z_hi, core), col: 16 (over z_lo, x).
Axes of the slice: x: 4, y: 4, z: 8 (z_hi: 2, z_lo: 4; z = z_hi * 4 + z_lo), core: 2. Of those that a mesh axis runs over, the one named last changes fastest.
Arguments:
- iterate: float32 [5120, 12800], P('row', 'col'), may hold values from -0.03125 to 0.03125
Outputs:
- update: float32 [5120, 12800], P('row', 'col')
All inputs are finite; a program needn't handle non-finite values.
Results may differ from a plain program's by a relative error of at most 0.0043.
Values may be sent and summed in bfloat16 or wider, within the bound.
No kernel may reach another device: no remote copies, remote signals or barrier semaphores. Data moves between devices by JAX's collectives and lax.ppermute only.
A program may use at most 128 MiB of HBM per device.

v0:
```python
import math

import jax
import jax.numpy as jnp
from jax import lax
from jax.sharding import PartitionSpec as P

coef_a = 3.4445
coef_b = -4.775
coef_c = 2.0315


def transposed_product(left_part, right_part):
    return lax.dot_general(
        left_part, right_part, (((1,), (1,)), ((), ())), preferred_element_type=jnp.float32
    )


def local(iterate):
    row_count = lax.axis_size("row")
    col_count = lax.axis_size("col")
    col_index = lax.axis_index("col")
    local_rows = iterate.shape[0]
    local_cols = iterate.shape[1]
    total_rows = local_rows * row_count
    total_cols = local_cols * col_count
    tile_cols = total_rows // col_count
    narrow = iterate.astype(jnp.bfloat16)
    columns = lax.all_gather(narrow, "row", axis=0, tiled=True)
    partial_value = transposed_product(narrow, columns)
    gram_rows = lax.optimization_barrier(lax.psum(partial_value, "col").astype(jnp.bfloat16))
    gram_tile = lax.dynamic_slice_in_dim(gram_rows, col_index * tile_cols, tile_cols, 1)
    square = jnp.dot(
        gram_rows,
        lax.all_gather(gram_tile, "row", axis=0, tiled=True),
        preferred_element_type=jnp.float32,
    )
    mixing = (coef_b * gram_tile.astype(jnp.float32) + coef_c * square).astype(jnp.bfloat16)
    product = jnp.dot(
        lax.all_gather(mixing, "col", axis=1, tiled=True),
        columns,
        preferred_element_type=jnp.float32,
    )
    factor = 0.2 * math.sqrt(max(total_rows, total_cols))
    return factor * (coef_a * iterate + product)


def solution(mesh):
    placed = (P("row", "col"),)
    return jax.shard_map(
        local, mesh=mesh, in_specs=placed, out_specs=P("row", "col"), check_vma=False
    )
```

profile of v0, /device:TPU:2, one launch (start us, length us, event | category | flops | bytes accessed | tf_op | source)
XLA Modules:
  0.0 464.2 jit_solution(531223622535224649)
XLA Ops:
  6.5 0.0 all-gather.4.cloned.1.call-start
  6.5 2.1 convert_element_type.12
  8.7 0.0 all-gather.4.cloned.1.call-update
  8.7 0.0 all-gather.6.cloned.1.call-start
  8.7 115.4 %all-gather.4.cloned.1.call-done = bf16[5120,800]{1,0:T(8,128)(2,1)} async-done(((bf16[320,800]{1,0:T(8,128)(2,1)}), bf16[5120,800]{1,0:T(8,128)(2,1)}) %all-gather.4.cloned.1.call-update) | async-done | bytes 8192016 | tf_op jit(solution)/shard_map/all_gather | solution.py:29
  124.2 10.1 %fusion.3 = f32[320,5120]{1,0:T(8,128)} fusion(bf16[320,800]{1,0:T(8,128)(2,1)} %convert_element_type.12, bf16[5120,800]{1,0:T(8,128)(2,1)} %all-gather.4.cloned.1.call-done), kind=kOutput, calls=%fused_computation.6 | convolution fusion | flops 2621440000 | bytes 15257600 | tf_op jit(solution)/shard_map/dot_general | solution.py:14
  134.3 148.2 %all-reduce.1 = bf16[320,5120]{1,0:T(8,128)(2,1)S(1)} all-reduce(f32[320,5120]{1,0:T(8,128)} %fusion.3), channel_id=1, replica_groups=mesh['row'=16,'col'=16] {'col'}, use_global_device_ids=true, to_apply=%region_0.0 | all-reduce | flops 1638400 | bytes 9830400 | tf_op jit(solution)/shard_map/psum | solution.py:31
  282.6 0.0 copy-start.1
  282.6 1.0 constant_dynamic-slice_fusion
  283.6 0.7 copy-done.1
  284.3 0.0 all-gather.6.cloned.1.call-update
  284.3 0.0 copy-start
  284.3 0.0 all-gather.8.cloned.1.call-start
  284.4 75.0 %all-gather.6.cloned.1.call-done = bf16[5120,320]{1,0:T(8,128)(2,1)} async-done(((bf16[320,320]{1,0:T(8,128)(2,1)}), bf16[5120,320]{1,0:T(8,128)(2,1)}) %all-gather.6.cloned.1.call-update) | async-done | bytes 3276816 | tf_op jit(solution)/shard_map/all_gather | solution.py:35
  359.4 5.0 %fusion.2 = bf16[320,320]{1,0:T(8,128)(2,1)S(1)} fusion(bf16[320,5120]{1,0:T(8,128)(2,1)} %copy-done.1, bf16[5120,320]{1,0:T(8,128)(2,1)} %all-gather.6.cloned.1.call-done, bf16[320,320]{1,0:T(8,128)(2,1)} %constant_dynamic-slice_fusion), kind=kOutput, calls=%fused_computation.4 | convolution fusion | flops 1049088000 | bytes 6963200 | tf_op jit(solution)/shard_map/dot_general | solution.py:33
  364.4 0.9 copy.2
  365.2 0.0 all-gather.8.cloned.1.call-update
  365.3 83.0 %all-gather.8.cloned.1.call-done = bf16[320,5120]{0,1:T(8,128)(2,1)} async-done(((bf16[320,320]{0,1:T(8,128)(2,1)}), bf16[320,5120]{0,1:T(8,128)(2,1)}) %all-gather.8.cloned.1.call-update) | async-done | bytes 3276816 | tf_op jit(solution)/shard_map/all_gather | solution.py:40
  448.3 0.0 copy-done
  448.3 9.4 %fusion = f32[320,800]{1,0:T(8,128)} fusion(bf16[320,5120]{0,1:T(8,128)(2,1)} %all-gather.8.cloned.1.call-done, bf16[5120,800]{1,0:T(8,128)(2,1)} %all-gather.4.cloned.1.call-done, f32[320,800]{1,0:T(8,128)S(1)} %copy-done), kind=kOutput, calls=%fused_computation.1 | convolution fusion | flops 2622208000 | bytes 13516800 | tf_op jit(solution)/shard_map/dot_general | solution.py:39
Async XLA Ops:
  6.5 117.6 %all-gather.4.cloned.1.call-start = ((), (), s32[]{:S(2)}) async-start(), calls=%async_computation | async-start | bytes 9748480 | tf_op jit(solution)/shard_map/all_gather | solution.py:29
  8.7 350.7 %all-gather.6.cloned.1.call-start = ((), (), s32[]{:S(2)}) async-start(), calls=%async_computation.1 | async-start | bytes 4177920 | tf_op jit(solution)/shard_map/all_gather | solution.py:35
  282.6 1.7 copy-start.1
  284.3 164.0 %copy-start = (f32[320,800]{1,0:T(8,128)S(1)}, f32[320,800]{1,0:T(8,128)}, u32[]{:S(2)}) copy-start(f32[320,800]{1,0:T(8,128)} %param.1) | copy-start | bytes 3072004
  284.3 164.0 %all-gather.8.cloned.1.call-start = ((), (), s32[]{:S(2)}) async-start(), calls=%async_computation.2 | async-start | bytes 4177920 | tf_op jit(solution)/shard_map/all_gather | solution.py:40
Sparse Core Ops, SparseCore 0:
  10.0 114.0 all-gather.3
  284.4 74.8 all-gather.5
  365.4 82.8 all-gather.7
where the time goes:
time: 464 us
  waiting for transfers between devices  274 us (59%)
  blocking collectives  148 us (32%)
  matrix products  24.5 us (5%)
  between operations  13.1 us (3%)
    psum x1, blocking collectives, local(): lax.psum(partial_value, 'col').astype(jnp.bfloat16)  148 us
    all_gather x1, waiting for transfers between devices, local(): columns = lax.all_gather(narrow, 'row', axis=0, tiled=True)  115 us
    all_gather x1, waiting for transfers between devices, local(): lax.all_gather(mixing, 'col', axis=1, tiled=True)  83 us
    all_gather x1, waiting for transfers between devices, local(): lax.all_gather(gram_tile, 'row', axis=0, tiled=True)  75 us
    dot_general x1, matrix products, transposed_product(): lax.dot_general(left_part, right_part, (((1,), (1,)), ((), ())), preferre...  10.1 us
    dot_general x1, matrix products, local(): jnp.dot(lax.all_gather(mixing, 'col', axis=1, tiled=True), columns, prefe...  9.39 us
  transfers between devices with their start and end apart: 3, of which 3 were waited for; matrix products, arithmetic and copies ran while one was open for 0% of the time, Pallas kernels for 0%

commit v1 on v0

v1 whole, which is shorter than its diff:
```python
import math

import jax
import jax.numpy as jnp
from jax import lax
from jax.sharding import PartitionSpec as P

coef_a = 3.4445
coef_b = -4.775
coef_c = 2.0315

axes = ("row", "col")


def fetch(value, source):
    pairs = []
    for row in range(16):
        for col in range(16):
            y, half, core, run, x = source(row // 4, row // 2 % 2, row % 2, col // 4, col % 4)
            pairs.append((((y * 2 + half) * 2 + core) * 16 + run * 4 + x, row * 16 + col))
    return lax.ppermute(value, axes, pairs)


def other_core(value):
    return fetch(value, lambda y, half, core, run, x: (y, half, 1 - core, run, x))


def other_half(value):
    return fetch(value, lambda y, half, core, run, x: (y, 1 - half, core, run, x))


def along_y(value, step):
    return fetch(value, lambda y, half, core, run, x: (y ^ x ^ step, half, core, run, x))


def along_run(value, step):
    return fetch(value, lambda y, half, core, run, x: (y, half, core, run ^ step, x))


def along_x(value, step):
    return fetch(value, lambda y, half, core, run, x: (y, half, core, run, x ^ step))


def gather_rows(block):
    found = {}
    for far, value in enumerate((block, other_half(block))):
        for step in range(4):
            found[step, far] = along_y(value, step)
    return found


def times(left, right):
    return jnp.dot(left, right, preferred_element_type=jnp.float32)


def times_transposed(left, right):
    return lax.dot_general(
        left, right, (((1,), (1,)), ((), ())), preferred_element_type=jnp.float32
    )


def total(values):
    summed = values[0].astype(jnp.float32)
    for value in values[1:]:
        summed = summed + value.astype(jnp.float32)
    return summed


def picked(stacked, index, rows):
    return lax.dynamic_slice_in_dim(stacked, index * rows, rows, 0)


def local(iterate):
    rows = iterate.shape[0]
    run = lax.axis_index("col") // 4
    total_rows = rows * lax.axis_size("row")
    total_cols = iterate.shape[1] * lax.axis_size("col")
    narrow = iterate.astype(jnp.bfloat16)
    chip_rows = jnp.concatenate([narrow, other_core(narrow)], axis=0)
    blocks = gather_rows(narrow)

    reduced = []
    for far in range(2):
        parts = []
        for step in range(4):
            part = times_transposed(chip_rows, blocks[step, far]).astype(jnp.bfloat16)
            parts.append(along_x(part, step) if step else part)
        reduced.append(total(parts).astype(jnp.bfloat16))
    reduced = jnp.concatenate(reduced, axis=0)
    parts = [picked(reduced, run ^ step, rows) for step in range(4)]
    tile = total([along_run(part, step) if step else part for step, part in enumerate(parts)])
    tile = tile.astype(jnp.bfloat16)

    tiles = jnp.concatenate(
        [along_run(tile, step) if step else tile for step in range(4)], axis=0
    )
    gram = {}
    for far in range(2):
        chunk = jnp.concatenate(
            [picked(tiles, run ^ (2 * far + core), rows) for core in range(2)], axis=0
        )
        for step in range(4):
            gram[step, far] = along_x(chunk, step) if step else chunk

    def multiplied(right):
        product = total([times(gram[key], right[key]) for key in gram])
        return product[:rows] + other_core(product[rows:].astype(jnp.bfloat16)).astype(jnp.float32)

    inner = coef_b * narrow.astype(jnp.float32) + coef_c * multiplied(blocks)
    product = multiplied(gather_rows(inner.astype(jnp.bfloat16)))
    factor = 0.2 * math.sqrt(max(total_rows, total_cols))
    return factor * (coef_a * iterate + product)


def solution(mesh):
    placed = (P("row", "col"),)
    return jax.shard_map(
        local, mesh=mesh, in_specs=placed, out_specs=P("row", "col"), check_vma=False
    )
```

time: 464 us -> 272 us (0.59)
  the two profiles are of different devices: /device:TPU:2 before, /device:TPU:33 now
where the time goes in v1:
time: 272 us; the launch traced here: 271 us
  waiting for transfers between devices  149 us (55%)
  starting transfers between devices  85.9 us (32%)
  matrix products  26.8 us (10%)
  other arithmetic  6.09 us (2%)
  local copies, waits for them, and re-layouts  2.75 us (1%)
    ppermute x39, waiting for transfers between devices, fetch(): return lax.ppermute(value, axes, pairs)  149 us
    ppermute x39, starting transfers between devices, fetch(): return lax.ppermute(value, axes, pairs)  85.9 us
    dot_general x16, matrix products, times(): return jnp.dot(left, right, preferred_element_type=jnp.float32)  15.7 us
    dot_general x8, matrix products, times_transposed(): lax.dot_general(left, right, (((1,), (1,)), ((), ())), preferred_element_...  11.1 us
  transfers between devices with their start and end apart: 39, of which 26 were waited for; matrix products, arithmetic and copies ran while one was open for 8% of the time, Pallas kernels for 0%

profile of v1, /device:TPU:33, one launch (start us, length us, event | category | flops | bytes accessed | tf_op | source)
XLA Modules:
  0.0 271.5 jit_solution(2933732780339589152)
XLA Ops:
  2.1 6.0 %collective-permute-start.8 = (bf16[320,800]{1,0:T(8,128)(2,1)S(1)}, bf16[320,800]{1,0:T(8,128)(2,1)}, u32[]{:S(2)}, u32[]{:S(2)}) collective-permute-start(bf16[320,800]{1,0:T(8,128)(2,1)S(1)} %convert_element_type.86), channel_id=1, source_target_pairs={{32,0},{33,1},{34,2},{35,3},{36,4},{37,5},{38,6},{39,7},{40,8},{41... | collective-permute-start | bytes 1536008 | tf_op jit(solution)/shard_map/ppermute | solution.py:21
  11.3 4.5 %collective-permute-start.4 = (bf16[320,800]{1,0:T(8,128)(2,1)S(1)}, bf16[320,800]{1,0:T(8,128)(2,1)S(1)}, u32[]{:S(2)}, u32[]{:S(2)}) collective-permute-start(bf16[320,800]{1,0:T(8,128)(2,1)S(1)} %convert_element_type.86), channel_id=1, source_target_pairs={{128,0},{193,1},{2,2},{67,3},{132,4},{197,5},{6,6},{71,7},{136,8},... | collective-permute-start | bytes 1536008 | tf_op jit(solution)/shard_map/ppermute | solution.py:21
  18.5 15.2 %collective-permute-done.8 = bf16[320,800]{1,0:T(8,128)(2,1)} collective-permute-done((bf16[320,800]{1,0:T(8,128)(2,1)S(1)}, bf16[320,800]{1,0:T(8,128)(2,1)}, u32[]{:S(2)}, u32[]{:S(2)}) %collective-permute-start.8) | collective-permute-done | bytes 512032 | tf_op jit(solution)/shard_map/ppermute | solution.py:21
  49.5 7.8 %collective-permute-start.5 = (bf16[640,320]{0,1:T(8,128)(2,1)S(1)}, bf16[640,320]{0,1:T(8,128)(2,1)}, u32[]{:S(2)}, u32[]{:S(2)}) collective-permute-start(bf16[640,320]{0,1:T(8,128)(2,1)S(1)} %convolution_convert_fusion.5), channel_id=1, source_target_pairs={{2,0},{3,1},{0,2},{1,3},{6,4},{7,5},{4,6},{5,7},{10,8},{11,9},{8,1... | collective-permute-start | bytes 1228808 | tf_op jit(solution)/shard_map/ppermute | solution.py:21
  58.8 5.6 %collective-permute-done.12 = bf16[320,800]{1,0:T(8,128)(2,1)S(1)} collective-permute-done((bf16[320,800]{1,0:T(8,128)(2,1)}, bf16[320,800]{1,0:T(8,128)(2,1)S(1)}, u32[]{:S(2)}, u32[]{:S(2)}) %collective-permute-start.12) | collective-permute-done | bytes 512032 | tf_op jit(solution)/shard_map/ppermute | solution.py:21
  67.8 6.0 %collective-permute-done.14 = bf16[320,800]{1,0:T(8,128)(2,1)S(1)} collective-permute-done((bf16[320,800]{1,0:T(8,128)(2,1)}, bf16[320,800]{1,0:T(8,128)(2,1)S(1)}, u32[]{:S(2)}, u32[]{:S(2)}) %collective-permute-start.14) | collective-permute-done | bytes 512032 | tf_op jit(solution)/shard_map/ppermute | solution.py:21
  73.7 5.9 %collective-permute-start.9 = (bf16[320,800]{1,0:T(8,128)(2,1)}, bf16[320,800]{1,0:T(8,128)(2,1)}, u32[]{:S(2)}, u32[]{:S(2)}) collective-permute-start(bf16[320,800]{1,0:T(8,128)(2,1)} %collective-permute-done.8), channel_id=1, source_target_pairs={{0,0},{65,1},{130,2},{195,3},{4,4},{69,5},{134,6},{199,7},{8,8},{7... | collective-permute-start | bytes 1536008 | tf_op jit(solution)/shard_map/ppermute | solution.py:21
  81.4 3.7 %collective-permute-start.15 = (bf16[640,320]{0,1:T(8,128)(2,1)}, bf16[640,320]{0,1:T(8,128)(2,1)}, u32[]{:S(2)}, u32[]{:S(2)}) collective-permute-start(bf16[640,320]{0,1:T(8,128)(2,1)} %convolution_convert_fusion), channel_id=1, source_target_pairs={{3,0},{2,1},{1,2},{0,3},{7,4},{6,5},{5,6},{4,7},{11,8},{10,9},{9,1... | collective-permute-start | bytes 1228808 | tf_op jit(solution)/shard_map/ppermute | solution.py:21
  90.4 6.9 %collective-permute-done.13 = bf16[640,320]{0,1:T(8,128)(2,1)} collective-permute-done((bf16[640,320]{0,1:T(8,128)(2,1)}, bf16[640,320]{0,1:T(8,128)(2,1)}, u32[]{:S(2)}, u32[]{:S(2)}) %collective-permute-start.13) | collective-permute-done | bytes 409632 | tf_op jit(solution)/shard_map/ppermute | solution.py:21
  97.3 6.2 %collective-permute-done.15 = bf16[640,320]{0,1:T(8,128)(2,1)} collective-permute-done((bf16[640,320]{0,1:T(8,128)(2,1)}, bf16[640,320]{0,1:T(8,128)(2,1)}, u32[]{:S(2)}, u32[]{:S(2)}) %collective-permute-start.15) | collective-permute-done | bytes 409632 | tf_op jit(solution)/shard_map/ppermute | solution.py:21
  109.8 7.8 %collective-permute-done.16 = bf16[320,320]{0,1:T(8,128)(2,1)} collective-permute-done((bf16[320,320]{0,1:T(8,128)(2,1)}, bf16[320,320]{0,1:T(8,128)(2,1)}, u32[]{:S(2)}, u32[]{:S(2)}) %collective-permute-start.16) | collective-permute-done | bytes 204832 | tf_op jit(solution)/shard_map/ppermute | solution.py:21
  120.5 10.5 %collective-permute-done.18 = bf16[320,320]{0,1:T(8,128)(2,1)} collective-permute-done((bf16[320,320]{0,1:T(8,128)(2,1)S(1)}, bf16[320,320]{0,1:T(8,128)(2,1)}, u32[]{:S(2)}, u32[]{:S(2)}) %collective-permute-start.18) | collective-permute-done | bytes 204832 | tf_op jit(solution)/shard_map/ppermute | solution.py:21
  135.3 3.8 %collective-permute-done.19 = bf16[320,320]{0,1:T(8,128)(2,1)S(1)} collective-permute-done((bf16[320,320]{0,1:T(8,128)(2,1)S(1)}, bf16[320,320]{0,1:T(8,128)(2,1)S(1)}, u32[]{:S(2)}, u32[]{:S(2)}) %collective-permute-start.19) | collective-permute-done | bytes 204832 | tf_op jit(solution)/shard_map/ppermute | solution.py:21
  139.1 5.6 %collective-permute-done.20 = bf16[320,320]{0,1:T(8,128)(2,1)S(1)} collective-permute-done((bf16[320,320]{0,1:T(8,128)(2,1)S(1)}, bf16[320,320]{0,1:T(8,128)(2,1)S(1)}, u32[]{:S(2)}, u32[]{:S(2)}) %collective-permute-start.20) | collective-permute-done | bytes 204832 | tf_op jit(solution)/shard_map/ppermute | solution.py:21
  145.4 9.8 %collective-permute-done.21 = bf16[320,320]{0,1:T(8,128)(2,1)} collective-permute-done((bf16[320,320]{0,1:T(8,128)(2,1)S(1)}, bf16[320,320]{0,1:T(8,128)(2,1)}, u32[]{:S(2)}, u32[]{:S(2)}) %collective-permute-start.21) | collective-permute-done | bytes 204832 | tf_op jit(solution)/shard_map/ppermute | solution.py:21
  157.4 3.7 %collective-permute-start.24 = (bf16[640,320]{0,1:T(8,128)(2,1)S(1)}, bf16[640,320]{0,1:T(8,128)(2,1)S(1)}, u32[]{:S(2)}, u32[]{:S(2)}) collective-permute-start(bf16[640,320]{0,1:T(8,128)(2,1)S(1)} %pad_maximum_fusion.1), channel_id=1, source_target_pairs={{3,0},{2,1},{1,2},{0,3},{7,4},{6,5},{5,6},{4,7},{11,8},{10,9},{9,1... | collective-permute-start | bytes 1228808 | tf_op jit(solution)/shard_map/ppermute | solution.py:21
  176.9 6.0 %collective-permute-done.25 = bf16[640,320]{0,1:T(8,128)(2,1)S(1)} collective-permute-done((bf16[640,320]{0,1:T(8,128)(2,1)S(1)}, bf16[640,320]{0,1:T(8,128)(2,1)S(1)}, u32[]{:S(2)}, u32[]{:S(2)}) %collective-permute-start.25) | collective-permute-done | bytes 409632 | tf_op jit(solution)/shard_map/ppermute | solution.py:21
  183.7 6.5 %collective-permute-done.26 = bf16[640,320]{0,1:T(8,128)(2,1)S(1)} collective-permute-done((bf16[640,320]{0,1:T(8,128)(2,1)S(1)}, bf16[640,320]{0,1:T(8,128)(2,1)S(1)}, u32[]{:S(2)}, u32[]{:S(2)}) %collective-permute-start.26) | collective-permute-done | bytes 409632 | tf_op jit(solution)/shard_map/ppermute | solution.py:21
  205.4 3.9 %collective-permute-start.31 = (bf16[320,800]{1,0:T(8,128)(2,1)S(1)}, bf16[320,800]{1,0:T(8,128)(2,1)S(1)}, u32[]{:S(2)}, u32[]{:S(2)}) collective-permute-start(bf16[320,800]{1,0:T(8,128)(2,1)S(1)} %fusion.14), channel_id=1, source_target_pairs={{128,0},{193,1},{2,2},{67,3},{132,4},{197,5},{6,6},{71,7},{136,8},... | collective-permute-start | bytes 1536008 | tf_op jit(solution)/shard_map/ppermute | solution.py:21
  209.4 3.7 %collective-permute-start.32 = (bf16[320,800]{1,0:T(8,128)(2,1)S(1)}, bf16[320,800]{1,0:T(8,128)(2,1)S(1)}, u32[]{:S(2)}, u32[]{:S(2)}) collective-permute-start(bf16[320,800]{1,0:T(8,128)(2,1)S(1)} %fusion.14), channel_id=1, source_target_pairs={{192,0},{129,1},{66,2},{3,3},{196,4},{133,5},{70,6},{7,7},{200,8},... | collective-permute-start | bytes 1536008 | tf_op jit(solution)/shard_map/ppermute | solution.py:21
  213.1 15.7 %collective-permute-done.33 = bf16[320,800]{1,0:T(8,128)(2,1)S(1)} collective-permute-done((bf16[320,800]{1,0:T(8,128)(2,1)S(1)}, bf16[320,800]{1,0:T(8,128)(2,1)S(1)}, u32[]{:S(2)}, u32[]{:S(2)}) %collective-permute-start.33) | collective-permute-done | bytes 512032 | tf_op jit(solution)/shard_map/ppermute | solution.py:21
  235.1 6.0 %collective-permute-start.37 = (bf16[320,800]{1,0:T(8,128)(2,1)S(1)}, bf16[320,800]{1,0:T(8,128)(2,1)S(1)}, u32[]{:S(2)}, u32[]{:S(2)}) collective-permute-start(bf16[320,800]{1,0:T(8,128)(2,1)S(1)} %collective-permute-done.33), channel_id=1, source_target_pairs={{192,0},{129,1},{66,2},{3,3},{196,4},{133,5},{70,6},{7,7},{200,8},... | collective-permute-start | bytes 1536008 | tf_op jit(solution)/shard_map/ppermute | solution.py:21
  246.4 9.8 %collective-permute-done.36 = bf16[320,800]{1,0:T(8,128)(2,1)S(1)} collective-permute-done((bf16[320,800]{1,0:T(8,128)(2,1)S(1)}, bf16[320,800]{1,0:T(8,128)(2,1)S(1)}, u32[]{:S(2)}, u32[]{:S(2)}) %collective-permute-start.36) | collective-permute-done | bytes 512032 | tf_op jit(solution)/shard_map/ppermute | solution.py:21
  257.0 8.5 %collective-permute-done.37 = bf16[320,800]{1,0:T(8,128)(2,1)S(1)} collective-permute-done((bf16[320,800]{1,0:T(8,128)(2,1)S(1)}, bf16[320,800]{1,0:T(8,128)(2,1)S(1)}, u32[]{:S(2)}, u32[]{:S(2)}) %collective-permute-start.37) | collective-permute-done | bytes 512032 | tf_op jit(solution)/shard_map/ppermute | solution.py:21
  (115 shorter events, 101.6 us)
Async XLA Ops:
  2.1 31.7 %collective-permute-start.8 = (bf16[320,800]{1,0:T(8,128)(2,1)S(1)}, bf16[320,800]{1,0:T(8,128)(2,1)}, u32[]{:S(2)}, u32[]{:S(2)}) collective-permute-start(bf16[320,800]{1,0:T(8,128)(2,1)S(1)} %convert_element_type.86), channel_id=1, source_target_pairs={{32,0},{33,1},{34,2},{35,3},{36,4},{37,5},{38,6},{39,7},{40,8},{41... | collective-permute-start | bytes 1536008 | tf_op jit(solution)/shard_map/ppermute | solution.py:21
  8.1 28.8 %collective-permute-start.2 = (bf16[320,800]{1,0:T(8,128)(2,1)S(1)}, bf16[320,800]{1,0:T(8,128)(2,1)S(1)}, u32[]{:S(2)}, u32[]{:S(2)}) collective-permute-start(bf16[320,800]{1,0:T(8,128)(2,1)S(1)} %convert_element_type.86), channel_id=1, source_target_pairs={{64,0},{1,1},{194,2},{131,3},{68,4},{5,5},{198,6},{135,7},{72,8},{... | collective-permute-start | bytes 1536008 | tf_op jit(solution)/shard_map/ppermute | solution.py:21
  11.3 27.7 %collective-permute-start.4 = (bf16[320,800]{1,0:T(8,128)(2,1)S(1)}, bf16[320,800]{1,0:T(8,128)(2,1)S(1)}, u32[]{:S(2)}, u32[]{:S(2)}) collective-permute-start(bf16[320,800]{1,0:T(8,128)(2,1)S(1)} %convert_element_type.86), channel_id=1, source_target_pairs={{128,0},{193,1},{2,2},{67,3},{132,4},{197,5},{6,6},{71,7},{136,8},... | collective-permute-start | bytes 1536008 | tf_op jit(solution)/shard_map/ppermute | solution.py:21
  15.9 29.0 %collective-permute-start.6 = (bf16[320,800]{1,0:T(8,128)(2,1)S(1)}, bf16[320,800]{1,0:T(8,128)(2,1)S(1)}, u32[]{:S(2)}, u32[]{:S(2)}) collective-permute-start(bf16[320,800]{1,0:T(8,128)(2,1)S(1)} %convert_element_type.86), channel_id=1, source_target_pairs={{192,0},{129,1},{66,2},{3,3},{196,4},{133,5},{70,6},{7,7},{200,8},... | collective-permute-start | bytes 1536008 | tf_op jit(solution)/shard_map/ppermute | solution.py:21
  17.8 63.3 %collective-permute-start.1 = (bf16[320,800]{1,0:T(8,128)(2,1)S(1)}, bf16[320,800]{1,0:T(8,128)(2,1)S(1)}, u32[]{:S(2)}, u32[]{:S(2)}) collective-permute-start(bf16[320,800]{1,0:T(8,128)(2,1)S(1)} %convert_element_type.86), channel_id=1, source_target_pairs={{0,0},{65,1},{130,2},{195,3},{4,4},{69,5},{134,6},{199,7},{8,8},{7... | collective-permute-start | bytes 1536008 | tf_op jit(solution)/shard_map/ppermute | solution.py:21
  37.7 43.6 %collective-permute-start.3 = (bf16[640,320]{0,1:T(8,128)(2,1)S(1)}, bf16[640,320]{0,1:T(8,128)(2,1)}, u32[]{:S(2)}, u32[]{:S(2)}) collective-permute-start(bf16[640,320]{0,1:T(8,128)(2,1)S(1)} %convolution_convert_fusion.6), channel_id=1, source_target_pairs={{1,0},{0,1},{3,2},{2,3},{5,4},{4,5},{7,6},{6,7},{9,8},{8,9},{11,10... | collective-permute-start | bytes 1228808 | tf_op jit(solution)/shard_map/ppermute | solution.py:21
  39.0 25.4 %collective-permute-start.12 = (bf16[320,800]{1,0:T(8,128)(2,1)}, bf16[320,800]{1,0:T(8,128)(2,1)S(1)}, u32[]{:S(2)}, u32[]{:S(2)}) collective-permute-start(bf16[320,800]{1,0:T(8,128)(2,1)} %collective-permute-done.8), channel_id=1, source_target_pairs={{128,0},{193,1},{2,2},{67,3},{132,4},{197,5},{6,6},{71,7},{136,8},... | collective-permute-start | bytes 1536008 | tf_op jit(solution)/shard_map/ppermute | solution.py:21
  44.8 28.9 %collective-permute-start.14 = (bf16[320,800]{1,0:T(8,128)(2,1)}, bf16[320,800]{1,0:T(8,128)(2,1)S(1)}, u32[]{:S(2)}, u32[]{:S(2)}) collective-permute-start(bf16[320,800]{1,0:T(8,128)(2,1)} %collective-permute-done.8), channel_id=1, source_target_pairs={{192,0},{129,1},{66,2},{3,3},{196,4},{133,5},{70,6},{7,7},{200,8},... | collective-permute-start | bytes 1536008 | tf_op jit(solution)/shard_map/ppermute | solution.py:21
  49.5 31.8 %collective-permute-start.5 = (bf16[640,320]{0,1:T(8,128)(2,1)S(1)}, bf16[640,320]{0,1:T(8,128)(2,1)}, u32[]{:S(2)}, u32[]{:S(2)}) collective-permute-start(bf16[640,320]{0,1:T(8,128)(2,1)S(1)} %convolution_convert_fusion.5), channel_id=1, source_target_pairs={{2,0},{3,1},{0,2},{1,3},{6,4},{7,5},{4,6},{5,7},{10,8},{11,9},{8,1... | collective-permute-start | bytes 1228808 | tf_op jit(solution)/shard_map/ppermute | solution.py:21
  64.4 20.7 %collective-permute-start.7 = (bf16[640,320]{0,1:T(8,128)(2,1)S(1)}, bf16[640,320]{0,1:T(8,128)(2,1)}, u32[]{:S(2)}, u32[]{:S(2)}) collective-permute-start(bf16[640,320]{0,1:T(8,128)(2,1)S(1)} %convolution_convert_fusion.4), channel_id=1, source_target_pairs={{3,0},{2,1},{1,2},{0,3},{7,4},{6,5},{5,6},{4,7},{11,8},{10,9},{9,1... | collective-permute-start | bytes 1228808 | tf_op jit(solution)/shard_map/ppermute | solution.py:21
  81.4 22.2 %collective-permute-start.15 = (bf16[640,320]{0,1:T(8,128)(2,1)}, bf16[640,320]{0,1:T(8,128)(2,1)}, u32[]{:S(2)}, u32[]{:S(2)}) collective-permute-start(bf16[640,320]{0,1:T(8,128)(2,1)} %convolution_convert_fusion), channel_id=1, source_target_pairs={{3,0},{2,1},{1,2},{0,3},{7,4},{6,5},{5,6},{4,7},{11,8},{10,9},{9,1... | collective-permute-start | bytes 1228808 | tf_op jit(solution)/shard_map/ppermute | solution.py:21
  109.3 21.7 %collective-permute-start.18 = (bf16[320,320]{0,1:T(8,128)(2,1)S(1)}, bf16[320,320]{0,1:T(8,128)(2,1)}, u32[]{:S(2)}, u32[]{:S(2)}) collective-permute-start(bf16[320,320]{0,1:T(8,128)(2,1)S(1)} %get-tuple-element.11), channel_id=1, source_target_pairs={{12,0},{13,1},{14,2},{15,3},{8,4},{9,5},{10,6},{11,7},{4,8},{5,9},... | collective-permute-start | bytes 614408 | tf_op jit(solution)/shard_map/ppermute | solution.py:21
  135.0 20.1 %collective-permute-start.21 = (bf16[320,320]{0,1:T(8,128)(2,1)S(1)}, bf16[320,320]{0,1:T(8,128)(2,1)}, u32[]{:S(2)}, u32[]{:S(2)}) collective-permute-start(bf16[320,320]{0,1:T(8,128)(2,1)S(1)} %add_convert_fusion), channel_id=1, source_target_pairs={{12,0},{13,1},{14,2},{15,3},{8,4},{9,5},{10,6},{11,7},{4,8},{5,9},... | collective-permute-start | bytes 614408 | tf_op jit(solution)/shard_map/ppermute | solution.py:21
  157.4 18.6 %collective-permute-start.24 = (bf16[640,320]{0,1:T(8,128)(2,1)S(1)}, bf16[640,320]{0,1:T(8,128)(2,1)S(1)}, u32[]{:S(2)}, u32[]{:S(2)}) collective-permute-start(bf16[640,320]{0,1:T(8,128)(2,1)S(1)} %pad_maximum_fusion.1), channel_id=1, source_target_pairs={{3,0},{2,1},{1,2},{0,3},{7,4},{6,5},{5,6},{4,7},{11,8},{10,9},{9,1... | collective-permute-start | bytes 1228808 | tf_op jit(solution)/shard_map/ppermute | solution.py:21
  161.3 21.6 %collective-permute-start.25 = (bf16[640,320]{0,1:T(8,128)(2,1)S(1)}, bf16[640,320]{0,1:T(8,128)(2,1)S(1)}, u32[]{:S(2)}, u32[]{:S(2)}) collective-permute-start(bf16[640,320]{0,1:T(8,128)(2,1)S(1)} %pad_maximum_fusion.2), channel_id=1, source_target_pairs={{1,0},{0,1},{3,2},{2,3},{5,4},{4,5},{7,6},{6,7},{9,8},{8,9},{11,10... | collective-permute-start | bytes 1228808 | tf_op jit(solution)/shard_map/ppermute | solution.py:21
  161.4 28.9 %collective-permute-start.26 = (bf16[640,320]{0,1:T(8,128)(2,1)S(1)}, bf16[640,320]{0,1:T(8,128)(2,1)S(1)}, u32[]{:S(2)}, u32[]{:S(2)}) collective-permute-start(bf16[640,320]{0,1:T(8,128)(2,1)S(1)} %pad_maximum_fusion.2), channel_id=1, source_target_pairs={{2,0},{3,1},{0,2},{1,3},{6,4},{7,5},{4,6},{5,7},{10,8},{11,9},{8,1... | collective-permute-start | bytes 1228808 | tf_op jit(solution)/shard_map/ppermute | solution.py:21
  165.3 29.5 %collective-permute-start.27 = (bf16[640,320]{0,1:T(8,128)(2,1)S(1)}, bf16[640,320]{0,1:T(8,128)(2,1)S(1)}, u32[]{:S(2)}, u32[]{:S(2)}) collective-permute-start(bf16[640,320]{0,1:T(8,128)(2,1)S(1)} %pad_maximum_fusion.2), channel_id=1, source_target_pairs={{3,0},{2,1},{1,2},{0,3},{7,4},{6,5},{5,6},{4,7},{11,8},{10,9},{9,1... | collective-permute-start | bytes 1228808 | tf_op jit(solution)/shard_map/ppermute | solution.py:21
  201.3 27.6 %collective-permute-start.33 = (bf16[320,800]{1,0:T(8,128)(2,1)S(1)}, bf16[320,800]{1,0:T(8,128)(2,1)S(1)}, u32[]{:S(2)}, u32[]{:S(2)}) collective-permute-start(bf16[320,800]{1,0:T(8,128)(2,1)S(1)} %fusion.14), channel_id=1, source_target_pairs={{32,0},{33,1},{34,2},{35,3},{36,4},{37,5},{38,6},{39,7},{40,8},{41... | collective-permute-start | bytes 1536008 | tf_op jit(solution)/shard_map/ppermute | solution.py:21
  202.8 26.7 %collective-permute-start.30 = (bf16[320,800]{1,0:T(8,128)(2,1)S(1)}, bf16[320,800]{1,0:T(8,128)(2,1)S(1)}, u32[]{:S(2)}, u32[]{:S(2)}) collective-permute-start(bf16[320,800]{1,0:T(8,128)(2,1)S(1)} %fusion.14), channel_id=1, source_target_pairs={{64,0},{1,1},{194,2},{131,3},{68,4},{5,5},{198,6},{135,7},{72,8},{... | collective-permute-start | bytes 1536008 | tf_op jit(solution)/shard_map/ppermute | solution.py:21
  204.7 27.6 %collective-permute-start.29 = (bf16[320,800]{1,0:T(8,128)(2,1)S(1)}, bf16[320,800]{1,0:T(8,128)(2,1)S(1)}, u32[]{:S(2)}, u32[]{:S(2)}) collective-permute-start(bf16[320,800]{1,0:T(8,128)(2,1)S(1)} %fusion.14), channel_id=1, source_target_pairs={{0,0},{65,1},{130,2},{195,3},{4,4},{69,5},{134,6},{199,7},{8,8},{7... | collective-permute-start | bytes 1536008 | tf_op jit(solution)/shard_map/ppermute | solution.py:21
  205.4 29.7 %collective-permute-start.31 = (bf16[320,800]{1,0:T(8,128)(2,1)S(1)}, bf16[320,800]{1,0:T(8,128)(2,1)S(1)}, u32[]{:S(2)}, u32[]{:S(2)}) collective-permute-start(bf16[320,800]{1,0:T(8,128)(2,1)S(1)} %fusion.14), channel_id=1, source_target_pairs={{128,0},{193,1},{2,2},{67,3},{132,4},{197,5},{6,6},{71,7},{136,8},... | collective-permute-start | bytes 1536008 | tf_op jit(solution)/shard_map/ppermute | solution.py:21
  209.4 32.6 %collective-permute-start.32 = (bf16[320,800]{1,0:T(8,128)(2,1)S(1)}, bf16[320,800]{1,0:T(8,128)(2,1)S(1)}, u32[]{:S(2)}, u32[]{:S(2)}) collective-permute-start(bf16[320,800]{1,0:T(8,128)(2,1)S(1)} %fusion.14), channel_id=1, source_target_pairs={{192,0},{129,1},{66,2},{3,3},{196,4},{133,5},{70,6},{7,7},{200,8},... | collective-permute-start | bytes 1536008 | tf_op jit(solution)/shard_map/ppermute | solution.py:21
  232.3 23.8 %collective-permute-start.36 = (bf16[320,800]{1,0:T(8,128)(2,1)S(1)}, bf16[320,800]{1,0:T(8,128)(2,1)S(1)}, u32[]{:S(2)}, u32[]{:S(2)}) collective-permute-start(bf16[320,800]{1,0:T(8,128)(2,1)S(1)} %collective-permute-done.33), channel_id=1, source_target_pairs={{128,0},{193,1},{2,2},{67,3},{132,4},{197,5},{6,6},{71,7},{136,8},... | collective-permute-start | bytes 1536008 | tf_op jit(solution)/shard_map/ppermute | solution.py:21
  235.1 30.3 %collective-permute-start.37 = (bf16[320,800]{1,0:T(8,128)(2,1)S(1)}, bf16[320,800]{1,0:T(8,128)(2,1)S(1)}, u32[]{:S(2)}, u32[]{:S(2)}) collective-permute-start(bf16[320,800]{1,0:T(8,128)(2,1)S(1)} %collective-permute-done.33), channel_id=1, source_target_pairs={{192,0},{129,1},{66,2},{3,3},{196,4},{133,5},{70,6},{7,7},{200,8},... | collective-permute-start | bytes 1536008 | tf_op jit(solution)/shard_map/ppermute | solution.py:21
  (28 other events, 428.7 us)
